TPU v7x, 512 devices: a whole 4x4x16 slice. The times are simulated.
512 devices in a mesh: blk: 64 (over y, x, z_hi, core), layer: 8 (over z_lo).
Axes of the slice: x: 4, y: 4, z: 16 (z_hi: 2, z_lo: 8; z = z_hi * 8 + z_lo), core: 2. Of those that a mesh axis runs over, the one named last changes fastest.
Arguments:
- train_factors: bfloat16 [768, 8, 2, 64, 1024], P('blk', 'layer'), may hold values from -0.29882812 to 0.29882812
- val_factors: bfloat16 [256, 8, 2, 64, 1024], P('blk', 'layer'), may hold values from -0.29882812 to 0.29882812
Outputs:
- scores: float32 [768, 3, 4], P('blk')
All inputs are finite; a program needn't handle non-finite values.
Results may differ from a plain program's by a relative error of at most 0.0003.
Values may be sent and summed in bfloat16 or wider, within the bound.
A program may use at most 64 MiB of HBM per device.

v0:
```python
import jax
import jax.numpy as jnp
from jax import lax
from jax.sharding import PartitionSpec as P

HOPS = 3


def shifted(block, axis, distance):
    devices = range(lax.axis_size(axis))
    route = [((i - distance) % len(devices), i) for i in devices]
    return lax.ppermute(block, axis, route)


def pair_scores(train, val):
    act_gram = jnp.einsum(
        "iltr,jlsr->ijlts", train[:, :, 0], val[:, :, 0], preferred_element_type=jnp.float32
    )
    grad_gram = jnp.einsum(
        "iltr,jlsr->ijlts", train[:, :, 1], val[:, :, 1], preferred_element_type=jnp.float32
    )
    return jnp.sum(act_gram * grad_gram, axis=(2, 3, 4))


def local(train_factors, val_factors):
    blocks = [val_factors]
    current = val_factors
    for hop in range(1, HOPS):
        current = shifted(current, "blk", 1)
        blocks.append(current)
    partial_rows = jnp.stack([pair_scores(train_factors, block) for block in blocks], axis=1)
    return lax.psum(partial_rows, "layer")


def solution(mesh):
    return jax.shard_map(
        local,
        mesh=mesh,
        in_specs=(P("blk", "layer", None, None, None), P("blk", "layer", None, None, None)),
        out_specs=P("blk", None, None),
        check_vma=False,
    )
```

profile of v0, /device:TPU:24, one launch (start us, length us, event | category | flops | bytes accessed | tf_op | source)
XLA Modules:
  0.0 155.2 jit_solution(4251315491996441822)
XLA Ops:
  0.0 0.0 copy-start
  0.0 1.4 copy.3
  1.4 0.0 copy-start.1
  1.4 2.2 %collective-permute-start = (bf16[4,1,2,64,1024]{4,3,0,2,1:T(8,128)(2,1)S(1)}, bf16[4,1,2,64,1024]{4,3,0,2,1:T(8,128)(2,1)S(1)}, u32[]{:S(2)}, u32[]{:S(2)}) collective-permute-start(bf16[4,1,2,64,1024]{4,3,0,2,1:T(8,128)(2,1)S(1)} %copy.3), channel_id=1, source_target_pairs={{504,0},{0,8},{8,16},{16,24},{24,32},{32,40},{40,48},{48,56},{56,6... | collective-permute-start | bytes 3145736 | tf_op jit(solution)/shard_map/ppermute | solution.py:12
  3.6 32.6 %collective-permute-done = bf16[4,1,2,64,1024]{4,3,0,2,1:T(8,128)(2,1)S(1)} collective-permute-done((bf16[4,1,2,64,1024]{4,3,0,2,1:T(8,128)(2,1)S(1)}, bf16[4,1,2,64,1024]{4,3,0,2,1:T(8,128)(2,1)S(1)}, u32[]{:S(2)}, u32[]{:S(2)}) %collective-permute-start) | collective-permute-done | bytes 1048608 | tf_op jit(solution)/shard_map/ppermute | solution.py:12
  36.2 27.7 %collective-permute-start.1 = (bf16[4,1,2,64,1024]{4,3,0,2,1:T(8,128)(2,1)S(1)}, bf16[4,1,2,64,1024]{4,3,0,2,1:T(8,128)(2,1)S(1)}, u32[]{:S(2)}, u32[]{:S(2)}) collective-permute-start(bf16[4,1,2,64,1024]{4,3,0,2,1:T(8,128)(2,1)S(1)} %collective-permute-done), channel_id=1, source_target_pairs={{504,0},{0,8},{8,16},{16,24},{24,32},{32,40},{40,48},{48,56},{56,6... | collective-permute-start | bytes 3145736 | tf_op jit(solution)/shard_map/ppermute | solution.py:12
  63.9 0.0 copy-done
  63.9 2.4 %fusion.4 = f32[4,64,12,64]{3,1,2,0:T(8,128)S(1)} fusion(bf16[12,1,2,64,1024]{4,3,2,1,0:T(8,128)(2,1)} %param.2, bf16[4,1,2,64,1024]{4,3,2,1,0:T(8,128)(2,1)S(1)} %copy-done), kind=kOutput, calls=%fused_computation.4 | convolution fusion | flops 402653184 | bytes 2883584 | tf_op jit(solution)/shard_map/iltr,jlsr->ijlts/dot_general | solution.py:19
  66.4 0.0 copy-done.1
  66.4 1.1 multiply_reduce_fusion.2
  67.5 1.0 fusion.2
  68.5 1.1 multiply_reduce_fusion.1
  69.7 47.1 %collective-permute-done.1 = bf16[4,1,2,64,1024]{4,3,0,2,1:T(8,128)(2,1)S(1)} collective-permute-done((bf16[4,1,2,64,1024]{4,3,0,2,1:T(8,128)(2,1)S(1)}, bf16[4,1,2,64,1024]{4,3,0,2,1:T(8,128)(2,1)S(1)}, u32[]{:S(2)}, u32[]{:S(2)}) %collective-permute-start.1) | collective-permute-done | bytes 1048608 | tf_op jit(solution)/shard_map/ppermute | solution.py:12
  116.8 1.0 fusion
  117.8 1.1 multiply_reduce_fusion
  118.9 36.3 %psum.7 = f32[12,3,4]{0,2,1:T(4,128)} all-reduce(f32[12,3,4]{0,2,1:T(4,128)S(1)} %pad_maximum_fusion), channel_id=1, replica_groups=mesh['blk'=64,'layer'=8] {'layer'}, use_global_device_ids=true, to_apply=%region_3.0 | all-reduce | flops 144 | bytes 1152 | tf_op jit(solution)/shard_map/psum | solution.py:32
  (1 shorter events, 0.0 us)
Async XLA Ops:
  0.0 63.9 %copy-start = (bf16[4,1,2,64,1024]{4,3,2,1,0:T(8,128)(2,1)S(1)}, bf16[4,1,2,64,1024]{4,3,2,1,0:T(8,128)(2,1)}, u32[]{:S(2)}) copy-start(bf16[4,1,2,64,1024]{4,3,2,1,0:T(8,128)(2,1)} %param.3) | copy-start | bytes 3145732
  1.4 64.9 %copy-start.1 = (bf16[12,1,2,64,1024]{4,3,2,1,0:T(8,128)(2,1)S(1)}, bf16[12,1,2,64,1024]{4,3,2,1,0:T(8,128)(2,1)}, u32[]{:S(2)}) copy-start(bf16[12,1,2,64,1024]{4,3,2,1,0:T(8,128)(2,1)} %param.2) | copy-start | bytes 9437188
  1.4 34.8 %collective-permute-start = (bf16[4,1,2,64,1024]{4,3,0,2,1:T(8,128)(2,1)S(1)}, bf16[4,1,2,64,1024]{4,3,0,2,1:T(8,128)(2,1)S(1)}, u32[]{:S(2)}, u32[]{:S(2)}) collective-permute-start(bf16[4,1,2,64,1024]{4,3,0,2,1:T(8,128)(2,1)S(1)} %copy.3), channel_id=1, source_target_pairs={{504,0},{0,8},{8,16},{16,24},{24,32},{32,40},{40,48},{48,56},{56,6... | collective-permute-start | bytes 3145736 | tf_op jit(solution)/shard_map/ppermute | solution.py:12
  36.2 80.5 %collective-permute-start.1 = (bf16[4,1,2,64,1024]{4,3,0,2,1:T(8,128)(2,1)S(1)}, bf16[4,1,2,64,1024]{4,3,0,2,1:T(8,128)(2,1)S(1)}, u32[]{:S(2)}, u32[]{:S(2)}) collective-permute-start(bf16[4,1,2,64,1024]{4,3,0,2,1:T(8,128)(2,1)S(1)} %collective-permute-done), channel_id=1, source_target_pairs={{504,0},{0,8},{8,16},{16,24},{24,32},{32,40},{40,48},{48,56},{56,6... | collective-permute-start | bytes 3145736 | tf_op jit(solution)/shard_map/ppermute | solution.py:12
where the time goes:
time: 155 us
  waiting for transfers between devices  79.7 us (51%)
  blocking collectives  36.3 us (23%)
  starting transfers between devices  29.9 us (19%)
  matrix products  7.82 us (5%)
    ppermute x2, waiting for transfers between devices, shifted(): return lax.ppermute(block, axis, route)  79.7 us
    psum x1, blocking collectives, local(): return lax.psum(partial_rows, 'layer')  36.3 us
    ppermute x2, starting transfers between devices, shifted(): return lax.ppermute(block, axis, route)  29.9 us
    dot_general x3, matrix products, pair_scores(): jnp.einsum('iltr,jlsr->ijlts', train[:, :, 1], val[:, :, 1], preferred_el...  4.41 us
    dot_general x3, matrix products, pair_scores(): jnp.einsum('iltr,jlsr->ijlts', train[:, :, 0], val[:, :, 0], preferred_el...  3.41 us
  transfers between devices with their start and end apart: 2, of which 2 were waited for; matrix products, arithmetic and copies ran while one was open for 4% of the time, Pallas kernels for 0%

commit v1 on v0

v1 whole, which is shorter than its diff:
```python
import jax
import jax.numpy as jnp
from jax import lax
from jax.experimental import pallas as pl
from jax.experimental.pallas import tpu as pltpu
from jax.sharding import PartitionSpec as P

MESH = pl.DeviceIdType.MESH
TRAIN_DEV = 12
VAL_DEV = 4
HOPS = 3
TOK = 64
R = 1024
LAYERS = 8
RING = 16
STEPS = 8
COLUMNS = 16
N_BLK = 64
OWN, SIBLING, FIRST = 0, 1, 2
ARRIVED = FIRST + STEPS - 1


def chip(column, z, core):
    column, z = lax.rem(column + COLUMNS, COLUMNS), lax.rem(z + RING, RING)
    return (column * 2 + z // LAYERS) * 2 + core, lax.rem(z, LAYERS)


def kernel(train, val, out, tokens, held, total, parts, load_sem, send_sem, recv_sem, sib_send, sib_recv, sum_send, sum_recv):
    blk, layer = lax.axis_index("blk"), lax.axis_index("layer")
    core, column = lax.rem(blk, 2), blk // 4
    z = lax.rem(blk // 2, 2) * LAYERS + layer
    target = (
        chip(column + (z == RING - 1).astype(jnp.int32), z + 1, core),
        chip(column + (z == LAYERS).astype(jnp.int32), z - 1, core),
    )
    source = (
        chip(column - (z == 0).astype(jnp.int32), z - 1, core),
        chip(column - (z == LAYERS - 1).astype(jnp.int32), z + 1, core),
    )
    sibling = (blk + 1 - 2 * core, layer)

    barrier = pltpu.get_barrier_semaphore()
    for device in (*source, sibling):
        pl.semaphore_signal(barrier, inc=1, device_id=device, device_id_type=MESH)
    pl.semaphore_wait(barrier, 3)

    def ring(step, d, p, g):
        rows = pl.ds(d * TOK, TOK)
        if isinstance(step, int) and step == 0:
            src = val.at[2 * d + p, g]
        else:
            src = held.at[FIRST + step - 1, p, g, rows]
        return pltpu.make_async_remote_copy(
            src,
            held.at[FIRST + step, p, g, rows],
            send_sem.at[step, d, p, g],
            recv_sem.at[step, d, p, g],
            device_id=target[d],
            device_id_type=MESH,
        )

    chunks = [(p, g) for p in range(2) for g in range(2)]
    for p, g in chunks:
        for d in range(2):
            ring(0, d, p, g).start()

    own = [
        pltpu.make_async_copy(
            val.at[2 * d + p, g], held.at[OWN, p, g, pl.ds(d * TOK, TOK)], load_sem.at[2 + d, p, g]
        )
        for p, g in chunks
        for d in range(2)
    ]
    for copy in own:
        copy.start()
    factors = [
        pltpu.make_async_copy(train.at[:, g], tokens.at[g], load_sem.at[0, 0, g]) for g in range(2)
    ]
    for copy in factors:
        copy.start()

    def to_sibling(slot, p, g):
        return pltpu.make_async_remote_copy(
            held.at[slot, p, g],
            held.at[SIBLING, p, g],
            sib_send.at[p, g],
            sib_recv.at[p, g],
            device_id=sibling,
            device_id_type=MESH,
        )

    total[...] = jnp.zeros_like(total)

    def gram(slot, p, g):
        return lax.dot_general(
            tokens[g].reshape(TRAIN_DEV * TOK, R),
            held[slot, p, g],
            (((1,), (1,)), ((), ())),
            preferred_element_type=jnp.float32,
        )

    def add_scores(slot, p, hop):
        product = gram(slot, p, 0) * gram(slot, p, 1)
        sums = jnp.sum(product.reshape(TRAIN_DEV, TOK, 2 * TOK), axis=1)
        lane = lax.broadcasted_iota(jnp.int32, sums.shape, 1)
        first = jnp.sum(jnp.where(lane < TOK, sums, 0.0), axis=1, keepdims=True)
        second = jnp.sum(jnp.where(lane < TOK, 0.0, sums), axis=1, keepdims=True)
        at = hop * VAL_DEV + p
        scores = jnp.where(lane == at, first, jnp.where(lane == at + 2, second, 0.0))
        total[pl.ds(0, TRAIN_DEV)] += scores

    for copy in own + factors:
        copy.wait()

    @pl.when(core == 0)
    def _():
        for p, g in chunks:
            to_sibling(OWN, p, g).start()

    def step_body(step, carry):
        for p, g in chunks:
            for d in range(2):
                ring(step - 1, d, p, g).wait_recv()
                ring(step, d, p, g).start()

        @pl.when(step >= 3)
        def _():
            for p, g in chunks:
                for d in range(2):
                    ring(step - 2, d, p, g).wait_send()

        @pl.when((core == 1) & (step == 3))
        def _():
            for p, g in chunks:
                to_sibling(OWN, p, g).wait_recv()

        @pl.when((step <= 2) | ((core == 1) & (step <= 4)))
        def _():
            turn = step - 1
            add_scores(turn // 2, lax.rem(turn, 2), turn // 2)

        return carry

    lax.fori_loop(1, STEPS, step_body, 0)

    for p in range(2):
        for g in range(2):
            for d in range(2):
                ring(STEPS - 1, d, p, g).wait_recv()

            @pl.when(core == 1)
            def _():
                to_sibling(ARRIVED, p, g).start()

        add_scores(ARRIVED, p, 2)

        @pl.when(core == 0)
        def _():
            for g in range(2):
                to_sibling(ARRIVED, p, g).wait_recv()
            add_scores(SIBLING, p, 1)

    parts[layer] = total[...]

    def share(peer):
        return pltpu.make_async_remote_copy(
            total,
            parts.at[layer],
            sum_send.at[peer],
            sum_recv.at[layer],
            device_id=(blk, peer),
            device_id_type=MESH,
        )

    def shared_by(peer):
        return pltpu.make_async_remote_copy(
            total,
            parts.at[peer],
            sum_send.at[peer],
            sum_recv.at[peer],
            device_id=(blk, peer),
            device_id_type=MESH,
        )

    for peer in range(LAYERS):

        @pl.when(peer != layer)
        def _():
            share(peer).start()

    for step in (0, STEPS - 2, STEPS - 1):
        for p, g in chunks:
            for d in range(2):
                ring(step, d, p, g).wait_send()
    for p, g in chunks:
        to_sibling(OWN, p, g).wait_send()

    for peer in range(LAYERS):

        @pl.when(peer != layer)
        def _():
            shared_by(peer).wait_recv()
            share(peer).wait_send()

    out[...] = jnp.sum(parts[...], axis=0)


def local(train_factors, val_factors):
    train = train_factors.reshape(TRAIN_DEV, 2, TOK, R)
    val = val_factors.reshape(VAL_DEV, 2, TOK, R)
    summed = pl.pallas_call(
        kernel,
        out_shape=jax.ShapeDtypeStruct((16, 128), jnp.float32),
        in_specs=[pl.BlockSpec(memory_space=pl.ANY)] * 2,
        out_specs=pl.BlockSpec(memory_space=pltpu.VMEM),
        scratch_shapes=[
            pltpu.VMEM((2, TRAIN_DEV, TOK, R), jnp.bfloat16),
            pltpu.VMEM((FIRST + STEPS, 2, 2, 2 * TOK, R), jnp.bfloat16),
            pltpu.VMEM((16, 128), jnp.float32),
            pltpu.VMEM((LAYERS, 16, 128), jnp.float32),
            pltpu.SemaphoreType.DMA((4, 2, 2)),
            pltpu.SemaphoreType.DMA((STEPS, 2, 2, 2)),
            pltpu.SemaphoreType.DMA((STEPS, 2, 2, 2)),
            pltpu.SemaphoreType.DMA((2, 2)),
            pltpu.SemaphoreType.DMA((2, 2)),
            pltpu.SemaphoreType.DMA((LAYERS,)),
            pltpu.SemaphoreType.DMA((LAYERS,)),
        ],
        compiler_params=pltpu.CompilerParams(
            collective_id=0, has_side_effects=True, vmem_limit_bytes=60 * 2**20
        ),
        name="score_ring",
    )(train, val)
    return summed[:TRAIN_DEV, : HOPS * VAL_DEV].reshape(TRAIN_DEV, HOPS, VAL_DEV)


def solution(mesh):
    return jax.shard_map(
        local,
        mesh=mesh,
        in_specs=(P("blk", "layer", None, None, None), P("blk", "layer", None, None, None)),
        out_specs=P("blk", None, None),
        check_vma=False,
    )
```

time: 155 us -> 117 us (0.75)
  Pallas kernels: 0 us -> 115 us
  waiting for transfers between devices: 79.7 us -> 0 us
  blocking collectives: 36.3 us -> 0 us
  starting transfers between devices: 29.9 us -> 0 us
  matrix products: 7.82 us -> 0 us
    pallas_call x0 -> x1, Pallas kernels: none -> 115 us  [local(): pl.pallas_call(kernel, out_shape=jax.ShapeDtypeStruct((16, 128), jnp.floa...]
    ppermute x2 -> x0, waiting for transfers between devices: 79.7 us -> none  [shifted(): return lax.ppermute(block, axis, route)]
    psum x1 -> x0, blocking collectives: 36.3 us -> none  [local(): return lax.psum(partial_rows, 'layer')]
    ppermute x2 -> x0, starting transfers between devices: 29.9 us -> none  [shifted(): return lax.ppermute(block, axis, route)]
    dot_general x6 -> x0, matrix products: 7.82 us -> none  [the longest x3 4.41 us: pair_scores(): jnp.einsum('iltr,jlsr->ijlts', train[:, :, 1], val[:, :, 1], preferred_el...]
  transfers between devices with their start and end apart: 2 -> 0, of which waited for: 2 -> 0; matrix products, arithmetic and copies ran while one was open for 4% -> 0% of each run, Pallas kernels for 0% -> 0%
where the time goes in v1:
time: 117 us; the launch traced here: 116 us
  Pallas kernels  115 us (98%)
  local copies, waits for them, and re-layouts  1.39 us (1%)
    pallas_call x1, Pallas kernels, local(): pl.pallas_call(kernel, out_shape=jax.ShapeDtypeStruct((16, 128), jnp.floa...  115 us

profile of v1, /device:TPU:24, one launch (start us, length us, event | category | flops | bytes accessed | tf_op | source)
XLA Modules:
  0.0 116.3 jit_solution(4280931031637958208)
XLA Ops:
  0.0 114.9 %score_ring.1 = f32[16,128]{1,0:T(8,128)} custom-call(bf16[12,2,64,1024]{3,2,1,0:T(8,128)(2,1)} %bitcast.5, bf16[4,2,64,1024]{3,2,1,0:T(8,128)(2,1)} %bitcast.6), custom_call_target="tpu_custom_call" | custom-call | tf_op jit(solution)/shard_map/score_ring/pallas_call | solution.py:211
  114.9 0.8 copy.4
  115.7 0.6 reshape.11

commit v2 on v1

v2 whole, which is shorter than its diff:
```python
import jax
import jax.numpy as jnp
from jax import lax
from jax.experimental import pallas as pl
from jax.experimental.pallas import tpu as pltpu
from jax.sharding import PartitionSpec as P

MESH = pl.DeviceIdType.MESH
TRAIN_DEV = 12
VAL_DEV = 4
HOPS = 3
TOK = 64
R = 1024
LAYERS = 8
RING = 16
STEPS = 8
COLUMNS = 16
SUMS = 16
OWN, SIBLING, FIRST = 0, 1, 2
ARRIVED = FIRST + STEPS - 1
UP, DOWN = 0, 1
CHUNKS = [(p, g) for p in range(2) for g in range(2)]
TURNED = [(1, 1)]


def chip(column, z, core):
    column, z = lax.rem(column + COLUMNS, COLUMNS), lax.rem(z + RING, RING)
    return (column * 2 + z // LAYERS) * 2 + core, lax.rem(z, LAYERS)


def kernel(
    train, val, out, tokens, held, turned, act_gram, total, parts,
    load_sem, send_sem, recv_sem, turned_send, turned_recv, sib_send, sib_recv, sum_send, sum_recv,
):
    blk, layer = lax.axis_index("blk"), lax.axis_index("layer")
    core, column = lax.rem(blk, 2), blk // 4
    z = lax.rem(blk // 2, 2) * LAYERS + layer
    sibling = (blk + 1 - 2 * core, layer)

    def target(step, d):
        if d == UP:
            crosses = ((z == 0) & (step >= 1)) | ((z == 9) & (step == 1))
            return chip(column + crosses.astype(jnp.int32), z + 1, core)
        crosses = ((z == 7) & (step >= 1)) | ((z == 14) & (step == 1))
        return chip(column + crosses.astype(jnp.int32), z - 1, core)

    barrier = pltpu.get_barrier_semaphore()

    def greet(device):
        pl.semaphore_signal(barrier, inc=1, device_id=device, device_id_type=MESH)

    greet(chip(column, z + 1, core))
    greet(chip(column, z - 1, core))
    greet(sibling)

    @pl.when((z == 1) | (z == 10))
    def _():
        greet(chip(column - 1, z - 1, core))

    @pl.when((z == 6) | (z == 13))
    def _():
        greet(chip(column - 1, z + 1, core))

    more = (z == 0) | (z == 9) | (z == 7) | (z == 14)
    pl.semaphore_wait(barrier, 3 + more.astype(jnp.int32))

    def ring(step, d, p, g):
        rows = pl.ds(d * TOK, TOK)
        if isinstance(step, int) and step == 0:
            src = val.at[2 * d + p, g]
        else:
            src = held.at[FIRST + step - 1, p, g, rows]
        return pltpu.make_async_remote_copy(
            src,
            held.at[FIRST + step, p, g, rows],
            send_sem.at[step, d, p, g],
            recv_sem.at[step, d, p, g],
            device_id=target(step, d),
            device_id_type=MESH,
        )

    def turn(which, step):
        p, g = TURNED[which]
        first = isinstance(step, int) and step == 0
        last = isinstance(step, int) and step == STEPS - 1
        return pltpu.make_async_remote_copy(
            val.at[2 + p, g] if first else turned.at[which],
            held.at[ARRIVED, p, g, pl.ds(TOK, TOK)] if last else turned.at[which],
            turned_send.at[which],
            turned_recv.at[which],
            device_id=target(step, UP),
            device_id_type=MESH,
        )

    def goes_down(step, p, g, use):
        if (p, g) in TURNED:
            pl.when(z + step != LAYERS)(use)
        else:
            use()

    def begin():
        for p, g in CHUNKS:
            ring(0, UP, p, g).start()
            goes_down(0, p, g, lambda: ring(0, DOWN, p, g).start())
        for which in range(len(TURNED)):
            pl.when(z == LAYERS)(lambda: turn(which, 0).start())

    @pl.when(core == 1)
    def _():
        begin()

    own = [
        pltpu.make_async_copy(
            val.at[2 * d + p, g], held.at[OWN, p, g, pl.ds(d * TOK, TOK)], load_sem.at[2 + d, p, g]
        )
        for p, g in CHUNKS
        for d in range(2)
    ]
    for copy in own:
        copy.start()
    @pl.when(core == 0)
    def _():
        for copy in own:
            copy.wait()
        begin()

    factors = [
        pltpu.make_async_copy(train.at[:, g], tokens.at[g], load_sem.at[0, 0, g]) for g in range(2)
    ]
    for copy in factors:
        copy.start()

    def to_sibling(slot, p, g):
        return pltpu.make_async_remote_copy(
            held.at[slot, p, g],
            held.at[SIBLING, p, g],
            sib_send.at[p, g],
            sib_recv.at[p, g],
            device_id=sibling,
            device_id_type=MESH,
        )

    total[...] = jnp.zeros_like(total)

    def gram(g, left, right):
        return lax.dot_general(
            tokens[g].reshape(TRAIN_DEV * TOK, R),
            jnp.concatenate([left[...], right[...]], axis=0),
            (((1,), (1,)), ((), ())),
            preferred_element_type=jnp.float32,
        )

    def put_scores(act, grad, rows):
        sums = jnp.sum((act * grad).reshape(TRAIN_DEV, TOK, 4 * TOK), axis=1)
        sums = jnp.concatenate([sums, jnp.zeros((SUMS - TRAIN_DEV, 4 * TOK), jnp.float32)], axis=0)
        sums = jnp.sum(sums.T.reshape(4, TOK, SUMS), axis=1)
        for i, row in enumerate(rows):
            total[row : row + 1, pl.ds(0, SUMS)] = sums[i : i + 1]

    @pl.when(core == 1)
    def _():
        for copy in own:
            copy.wait()

    for copy in factors:
        copy.wait()

    @pl.when(core == 0)
    def _():
        for p, g in CHUNKS:
            to_sibling(OWN, p, g).start()

    put_scores(*(gram(g, held.at[OWN, 0, g], held.at[OWN, 1, g]) for g in range(2)), (0, 2, 1, 3))

    def step_body(step, carry):
        for p, g in CHUNKS:
            ring(step - 1, UP, p, g).wait_recv()
            ring(step, UP, p, g).start()

            def pass_down():
                ring(step - 1, DOWN, p, g).wait_recv()
                ring(step, DOWN, p, g).start()

            goes_down(step, p, g, pass_down)

        for which in range(len(TURNED)):

            @pl.when(z == LAYERS + step)
            def _():
                turn(which, 0).wait_recv()

                @pl.when(step < STEPS - 1)
                def _():
                    turn(which, step).start()

                @pl.when(step == STEPS - 1)
                def _():
                    turn(which, STEPS - 1).start()

        @pl.when(step >= 3)
        def _():
            for p, g in CHUNKS:
                ring(step - 2, UP, p, g).wait_send()
                goes_down(step - 2, p, g, lambda: ring(step - 2, DOWN, p, g).wait_send())

        return carry

    lax.fori_loop(1, STEPS, step_body, 0)

    def arrive(p, g):
        ring(STEPS - 1, UP, p, g).wait_recv()
        goes_down(STEPS, p, g, lambda: ring(STEPS - 1, DOWN, p, g).wait_recv())
        if (p, g) in TURNED:
            pl.when(z == 0)(lambda: turn(TURNED.index((p, g)), STEPS - 1).wait_recv())

    for p in range(2):
        for g in range(2):

            @pl.when(core == 1)
            def _():
                arrive(p, g)
                to_sibling(ARRIVED, p, g).start()
                to_sibling(OWN, p, g).wait_recv()

            @pl.when(core == 0)
            def _():
                to_sibling(ARRIVED, p, g).wait_recv()
                arrive(p, g)

            left, right = held.at[SIBLING, p, g], held.at[ARRIVED, p, g]
            if g == 0:
                act_gram[...] = gram(g, left, right)
            else:
                one, two = VAL_DEV + p, 2 * VAL_DEV + p
                put_scores(act_gram[...], gram(g, left, right), (one, one + 2, two, two + 2))

    parts[layer] = total[...]

    def share(peer, sender):
        return pltpu.make_async_remote_copy(
            total,
            parts.at[sender],
            sum_send.at[peer],
            sum_recv.at[sender],
            device_id=(blk, peer),
            device_id_type=MESH,
        )

    for peer in range(LAYERS):

        @pl.when(peer != layer)
        def _():
            share(peer, layer).start()

    for step in (0, STEPS - 2, STEPS - 1):
        for p, g in CHUNKS:
            ring(step, UP, p, g).wait_send()
            goes_down(step, p, g, lambda: ring(step, DOWN, p, g).wait_send())
    for p, g in CHUNKS:
        to_sibling(OWN, p, g).wait_send()
    for which in range(len(TURNED)):
        pl.when(z >= LAYERS)(lambda: turn(which, 0).wait_send())

    for peer in range(LAYERS):

        @pl.when(peer != layer)
        def _():
            share(peer, peer).wait_recv()
            share(peer, layer).wait_send()

    out[...] = jnp.sum(parts[...], axis=0)


def local(train_factors, val_factors):
    train = train_factors.reshape(TRAIN_DEV, 2, TOK, R)
    val = val_factors.reshape(VAL_DEV, 2, TOK, R)
    summed = pl.pallas_call(
        kernel,
        out_shape=jax.ShapeDtypeStruct((SUMS, 128), jnp.float32),
        in_specs=[pl.BlockSpec(memory_space=pl.ANY)] * 2,
        out_specs=pl.BlockSpec(memory_space=pltpu.VMEM),
        scratch_shapes=[
            pltpu.VMEM((2, TRAIN_DEV, TOK, R), jnp.bfloat16),
            pltpu.VMEM((FIRST + STEPS, 2, 2, 2 * TOK, R), jnp.bfloat16),
            pltpu.VMEM((max(len(TURNED), 1), TOK, R), jnp.bfloat16),
            pltpu.VMEM((TRAIN_DEV * TOK, 4 * TOK), jnp.float32),
            pltpu.VMEM((SUMS, 128), jnp.float32),
            pltpu.VMEM((LAYERS, SUMS, 128), jnp.float32),
            pltpu.SemaphoreType.DMA((4, 2, 2)),
            pltpu.SemaphoreType.DMA((STEPS, 2, 2, 2)),
            pltpu.SemaphoreType.DMA((STEPS, 2, 2, 2)),
            pltpu.SemaphoreType.DMA((max(len(TURNED), 1),)),
            pltpu.SemaphoreType.DMA((max(len(TURNED), 1),)),
            pltpu.SemaphoreType.DMA((2, 2)),
            pltpu.SemaphoreType.DMA((2, 2)),
            pltpu.SemaphoreType.DMA((LAYERS,)),
            pltpu.SemaphoreType.DMA((LAYERS,)),
        ],
        compiler_params=pltpu.CompilerParams(
            collective_id=0, has_side_effects=True, vmem_limit_bytes=60 * 2**20
        ),
        name="score_ring",
    )(train, val)
    scores = summed[: HOPS * VAL_DEV, :TRAIN_DEV]
    return scores.reshape(HOPS, VAL_DEV, TRAIN_DEV).transpose(2, 0, 1)


def solution(mesh):
    return jax.shard_map(
        local,
        mesh=mesh,
        in_specs=(P("blk", "layer", None, None, None), P("blk", "layer", None, None, None)),
        out_specs=P("blk", None, None),
        check_vma=False,
    )
```

time: 117 us -> 113 us (0.966)
  Pallas kernels: 115 us -> 111 us
    pallas_call x1, Pallas kernels: 115 us -> 111 us  [local(): pl.pallas_call(kernel, out_shape=jax.ShapeDtypeStruct((SUMS, 128), jnp.fl...]
where the time goes in v2:
time: 113 us; the launch traced here: 112 us
  Pallas kernels  111 us (98%)
  local copies, waits for them, and re-layouts  1.3 us (1%)
    pallas_call x1, Pallas kernels, local(): pl.pallas_call(kernel, out_shape=jax.ShapeDtypeStruct((SUMS, 128), jnp.fl...  111 us

profile of v2, /device:TPU:24, one launch (start us, length us, event | category | flops | bytes accessed | tf_op | source)
XLA Modules:
  0.0 111.9 jit_solution(12532672867428907471)
XLA Ops:
  0.0 110.6 %score_ring.1 = f32[16,128]{1,0:T(8,128)} custom-call(bf16[12,2,64,1024]{3,2,1,0:T(8,128)(2,1)} %bitcast.4, bf16[4,2,64,1024]{3,2,1,0:T(8,128)(2,1)} %bitcast.5), custom_call_target="tpu_custom_call" | custom-call | tf_op jit(solution)/shard_map/score_ring/pallas_call | solution.py:277
  110.6 1.3 %reshape.11 = f32[3,4,12]{2,1,0:T(4,128)} reshape(f32[12,12]{1,0:T(8,128)} %bitcast.6) | data formatting | bytes 1152 | tf_op jit(solution)/shard_map/reshape | solution.py:305

commit v3 on v0

v3 whole, which is shorter than its diff:
```python
import jax
import jax.numpy as jnp
from jax import lax
from jax.experimental import pallas as pl
from jax.experimental.pallas import tpu as pltpu
from jax.sharding import PartitionSpec as P

MESH = pl.DeviceIdType.MESH
TRAIN_DEV = 12
VAL_DEV = 4
HOPS = 3
TOK = 64
R = 1024
LAYERS = 8
RING = 16
LAST = 7
COLUMNS = 16
SUMS = 16
UP, DOWN = 0, 1
OWN, OTHER = 0, 1
CHUNKS = [(p, g) for p in range(2) for g in range(2)]
TURNED = {UP: [(1, 0), (1, 1)], DOWN: [(1, 1)]}
TURN_AT = {UP: LAYERS, DOWN: RING - 1}
TURNS = max(len(TURNED[UP]), len(TURNED[DOWN]), 1)
HEAD = 2
ORDER = {UP: [(OWN, 0, 0), (OWN, 0, 1), (OTHER, 0, 0), (OTHER, 0, 1), (OTHER, 1, 0), (OTHER, 1, 1), (OWN, 1, 0), (OWN, 1, 1)], DOWN: [(OWN, 0, 0), (OWN, 0, 1), (OTHER, 0, 0), (OTHER, 0, 1), (OWN, 1, 0), (OWN, 1, 1), (OTHER, 1, 0), (OTHER, 1, 1)]}


def chip(column, z, core):
    column, z = lax.rem(column + COLUMNS, COLUMNS), lax.rem(z + RING, RING)
    return (column * 2 + z // LAYERS) * 2 + core, lax.rem(z, LAYERS)


def quarter(i):
    return pl.ds(i * TOK, TOK)


def kernel(
    train, val, out, tokens, own, held, last, turned, act_gram, total, parts, load_sem, stage_send, stage_recv, give_send,
    give_recv, send_sem, recv_sem, cross_recv, turned_send, turned_recv, pass_send, pass_recv, sum_send, sum_recv,
):
    blk, layer = lax.axis_index("blk"), lax.axis_index("layer")
    core, column = lax.rem(blk, 2), blk // 4
    z = lax.rem(blk // 2, 2) * LAYERS + layer
    sibling = (blk + 1 - 2 * core, layer)

    def remote(src, dst, sent, received, device):
        return pltpu.make_async_remote_copy(src, dst, sent, received, device_id=device, device_id_type=MESH)

    def target(step, d, on_core):
        if d == UP:
            crosses = ((z == 0) & (step >= 1)) | ((z == 9) & (step == 1))
            return chip(column + crosses.astype(jnp.int32), z + 1, on_core)
        crosses = ((z == 7) & (step >= 1)) | ((z == 14) & (step == 1))
        return chip(column + crosses.astype(jnp.int32), z - 1, on_core)

    barrier = pltpu.get_barrier_semaphore()

    def greet(device):
        pl.semaphore_signal(barrier, inc=1, device_id=device, device_id_type=MESH)

    @pl.when(core == 0)
    def _():
        greet(chip(column, z - 1, 0))
        greet(chip(column, z + 1, 1))

        @pl.when((z == 1) | (z == 10))
        def _():
            greet(chip(column - 1, z - 1, 0))

        @pl.when(z == 6)
        def _():
            greet(chip(column - 1, z + 1, 1))

    @pl.when(core == 1)
    def _():
        greet(chip(column, z + 1, 1))

        @pl.when((z == 6) | (z == 13))
        def _():
            greet(chip(column - 1, z + 1, 1))

    greet(sibling)
    more_up = (core == 0) & ((z == 0) | (z == 9))
    more_down = (core == 1) & ((z == 7) | (z == 14))
    last_down = (core == 1) & (z == 7)
    pl.semaphore_wait(
        barrier,
        2 + core + more_up.astype(jnp.int32) + more_down.astype(jnp.int32) + last_down.astype(jnp.int32),
    )

    def ring(step, d, which, p, g):
        first = isinstance(step, int) and step == 0
        src = val.at[2 * d + p, g] if first and which == OWN else held.at[step, which, p, g]
        on_core, received = d, recv_sem.at[step, which, p, g]
        if isinstance(step, int) and step == LAST:
            dst = last.at[p, g, quarter((2 if which == d else 0) + d)]
            if d == DOWN and which == OTHER:
                on_core, received = 0, cross_recv.at[p, g]
        else:
            dst = held.at[step + 1, which, p, g]
        return remote(src, dst, send_sem.at[step, which, p, g], received, target(step, d, on_core))

    def starts_at(step, d):
        return lax.rem(z - step + RING, RING) if d == UP else lax.rem(z + step, RING)

    def unless_turned(step, d, which, p, g, use):
        other_way = 1 - d
        if which == d and (p, g) in TURNED[other_way]:
            pl.when(starts_at(step, d) != TURN_AT[other_way])(use)
        else:
            use()

    def turn(i, step, d):
        p, g = TURNED[d][i]
        first = isinstance(step, int) and step == 0
        ends = isinstance(step, int) and step == LAST
        here = last.at[p, g, quarter(3 if d == UP else 2)]
        if first:
            src = val.at[2 + p, g] if d == UP else here
        else:
            src = turned.at[i]
        return remote(
            src, here if ends else turned.at[i], turned_send.at[i], turned_recv.at[i], target(step, d, 0 if ends else d)
        )

    def stage(p, g):
        half = 2 * (1 - core) + p
        return remote(val.at[half, g], held.at[0, OTHER, p, g], stage_send.at[p, g], stage_recv.at[p, g], sibling)

    def give(p, g, d):
        return remote(
            val.at[2 * d + p, g], last.at[p, g, quarter(2 + d)], give_send.at[p, g, d], give_recv.at[p, g, d], sibling
        )

    def hand_over(d, p, g):
        here = last.at[p, g, quarter(d)]
        return remote(here, here, pass_send.at[p, g], pass_recv.at[p, g], sibling)

    for d in range(2):

        @pl.when(core == d)
        def _():
            for which, p, g in ORDER[d][:HEAD]:
                unless_turned(0, d, which, p, g, lambda: ring(0, d, which, p, g).start())

    for p, g in CHUNKS:
        stage(p, g).start()
    loads = [pltpu.make_async_copy(val.at[:, g], own.at[g], load_sem.at[0, g]) for g in range(2)]
    loads += [pltpu.make_async_copy(train.at[:, g], tokens.at[g], load_sem.at[1, g]) for g in range(2)]
    for copy in loads:
        copy.start()

    for d in range(2):

        @pl.when(core == d)
        def _():
            for which, p, g in ORDER[d][HEAD:]:
                if which == OTHER:
                    stage(p, g).wait_recv()
                unless_turned(0, d, which, p, g, lambda: ring(0, d, which, p, g).start())
            if d == UP:
                for i in range(len(TURNED[UP])):
                    pl.when(z == TURN_AT[UP])(lambda: turn(i, 0, UP).start())
                for half in range(2):
                    for p, g in CHUNKS:
                        give(p, g, half).start()
            else:
                for p, g in CHUNKS:
                    give(p, g, 0).wait_recv()
                for i in range(len(TURNED[DOWN])):
                    pl.when(z == TURN_AT[DOWN])(lambda: turn(i, 0, DOWN).start())

    total[...] = jnp.zeros_like(total)

    def gram(g, rows):
        return lax.dot_general(
            tokens[g].reshape(TRAIN_DEV * TOK, R),
            rows,
            (((1,), (1,)), ((), ())),
            preferred_element_type=jnp.float32,
        )

    def put_scores(act, grad, rows):
        sums = jnp.sum((act * grad).reshape(TRAIN_DEV, TOK, 4 * TOK), axis=1)
        sums = jnp.concatenate([sums, jnp.zeros((SUMS - TRAIN_DEV, 4 * TOK), jnp.float32)], axis=0)
        sums = jnp.sum(sums.T.reshape(4, TOK, SUMS), axis=1)
        for i, row in enumerate(rows):
            total[pl.ds(row, 1), pl.ds(0, SUMS)] = sums[i : i + 1]

    for copy in loads:
        copy.wait()
    put_scores(*(gram(g, own[g].reshape(4 * TOK, R)) for g in range(2)), range(VAL_DEV))

    for d in range(2):

        @pl.when(core == d)
        def _():
            def step_body(step, carry):
                for which, p, g in ORDER[d]:

                    def send_on():
                        ring(step - 1, d, which, p, g).wait_recv()
                        ring(step, d, which, p, g).start()

                    unless_turned(step, d, which, p, g, send_on)
                for i in range(len(TURNED[d])):

                    @pl.when((starts_at(step, d) == TURN_AT[d]) & (z >= LAYERS))
                    def _():
                        turn(i, step, d).wait_recv()
                        turn(i, step, d).start()

                @pl.when(step >= 3)
                def _():
                    for which, p, g in ORDER[d]:
                        unless_turned(step - 2, d, which, p, g, lambda: ring(step - 2, d, which, p, g).wait_send())

                return carry

            lax.fori_loop(1, LAST, step_body, 0)
            for which, p, g in ORDER[d]:

                def send_on():
                    ring(LAST - 1, d, which, p, g).wait_recv()
                    ring(LAST, d, which, p, g).start()

                unless_turned(LAST, d, which, p, g, send_on)
            for i in range(len(TURNED[d])):

                @pl.when(z == (TURN_AT[d] + (LAST if d == UP else -LAST)))
                def _():
                    turn(i, 1, d).wait_recv()
                    turn(i, LAST, d).start()

    for p in range(2):

        @pl.when(core == 0)
        def _():
            for g in range(2):
                ring(LAST, UP, OTHER, p, g).wait_recv()
                hand_over(UP, p, g).start()

        @pl.when(core == 1)
        def _():
            for g in range(2):
                ring(LAST, DOWN, OWN, p, g).wait_recv()
                hand_over(DOWN, p, g).start()

        for g in range(2):

            @pl.when(core == 0)
            def _():
                hand_over(DOWN, p, g).wait_recv()
                for way in (DOWN, UP):
                    which = OTHER if way == DOWN else OWN
                    other_way = 1 - way
                    if (p, g) in TURNED[other_way]:
                        ends = 0 if other_way == UP else LAYERS - 1
                        i = TURNED[other_way].index((p, g))
                        pl.when(z == ends)(lambda: turn(i, LAST, other_way).wait_recv())
                        pl.when(z != ends)(lambda: ring(LAST, way, which, p, g).wait_recv())
                    else:
                        ring(LAST, way, which, p, g).wait_recv()

            @pl.when(core == 1)
            def _():
                hand_over(UP, p, g).wait_recv()
                give(p, g, 1).wait_recv()

            if g == 0:
                act_gram[...] = gram(g, last[p, g])
            else:
                one, two = (1 + core) * VAL_DEV + p, (2 - core) * VAL_DEV + p
                put_scores(act_gram[...], gram(g, last[p, g]), (one, one + 2, two, two + 2))

    parts[layer] = total[...]

    def share(peer, sender):
        return remote(total, parts.at[sender], sum_send.at[peer], sum_recv.at[sender], (blk, peer))

    for peer in range(LAYERS):

        @pl.when(peer != layer)
        def _():
            share(peer, layer).start()

    for d in range(2):

        @pl.when(core == d)
        def _():
            for step in (0, LAST - 2, LAST - 1, LAST):
                for which, p, g in ORDER[d]:
                    unless_turned(step, d, which, p, g, lambda: ring(step, d, which, p, g).wait_send())
            for p, g in CHUNKS:
                hand_over(d, p, g).wait_send()
            if d == UP:
                for p, g in CHUNKS:
                    for half in range(2):
                        give(p, g, half).wait_send()
            for i in range(len(TURNED[d])):
                pl.when(z >= LAYERS)(lambda: turn(i, 0, d).wait_send())

    for p, g in CHUNKS:
        stage(p, g).wait_send()

    for peer in range(LAYERS):

        @pl.when(peer != layer)
        def _():
            share(peer, peer).wait_recv()
            share(peer, layer).wait_send()

    out[...] = jnp.sum(parts[...], axis=0)


def local(train_factors, val_factors):
    train = train_factors.reshape(TRAIN_DEV, 2, TOK, R)
    val = val_factors.reshape(VAL_DEV, 2, TOK, R)
    dma = pltpu.SemaphoreType.DMA
    summed = pl.pallas_call(
        kernel,
        out_shape=jax.ShapeDtypeStruct((SUMS, 128), jnp.float32),
        in_specs=[pl.BlockSpec(memory_space=pl.ANY)] * 2,
        out_specs=pl.BlockSpec(memory_space=pltpu.VMEM),
        scratch_shapes=[
            pltpu.VMEM((2, TRAIN_DEV, TOK, R), jnp.bfloat16),
            pltpu.VMEM((2, VAL_DEV, TOK, R), jnp.bfloat16),
            pltpu.VMEM((LAST + 1, 2, 2, 2, TOK, R), jnp.bfloat16),
            pltpu.VMEM((2, 2, 4 * TOK, R), jnp.bfloat16),
            pltpu.VMEM((TURNS, TOK, R), jnp.bfloat16),
            pltpu.VMEM((TRAIN_DEV * TOK, 4 * TOK), jnp.float32),
            pltpu.VMEM((SUMS, 128), jnp.float32),
            pltpu.VMEM((LAYERS, SUMS, 128), jnp.float32),
            dma((2, 2)),
            dma((2, 2)),
            dma((2, 2)),
            dma((2, 2, 2)),
            dma((2, 2, 2)),
            dma((LAST + 1, 2, 2, 2)),
            dma((LAST + 1, 2, 2, 2)),
            dma((2, 2)),
            dma((TURNS,)),
            dma((TURNS,)),
            dma((2, 2)),
            dma((2, 2)),
            dma((LAYERS,)),
            dma((LAYERS,)),
        ],
        compiler_params=pltpu.CompilerParams(
            collective_id=0, has_side_effects=True, vmem_limit_bytes=60 * 2**20
        ),
        name="score_ring",
    )(train, val)
    scores = summed[: HOPS * VAL_DEV, :TRAIN_DEV]
    return scores.reshape(HOPS, VAL_DEV, TRAIN_DEV).transpose(2, 0, 1)


def solution(mesh):
    return jax.shard_map(
        local,
        mesh=mesh,
        in_specs=(P("blk", "layer", None, None, None), P("blk", "layer", None, None, None)),
        out_specs=P("blk", None, None),
        check_vma=False,
    )
```

time: 155 us -> 112 us (0.72)
  Pallas kernels: 0 us -> 110 us
  waiting for transfers between devices: 79.7 us -> 0 us
  blocking collectives: 36.3 us -> 0 us
  starting transfers between devices: 29.9 us -> 0 us
  matrix products: 7.82 us -> 0 us
    pallas_call x0 -> x1, Pallas kernels: none -> 110 us  [local(): pl.pallas_call(kernel, out_shape=jax.ShapeDtypeStruct((SUMS, 128), jnp.fl...]
    ppermute x2 -> x0, waiting for transfers between devices: 79.7 us -> none  [shifted(): return lax.ppermute(block, axis, route)]
    psum x1 -> x0, blocking collectives: 36.3 us -> none  [local(): return lax.psum(partial_rows, 'layer')]
    ppermute x2 -> x0, starting transfers between devices: 29.9 us -> none  [shifted(): return lax.ppermute(block, axis, route)]
    dot_general x6 -> x0, matrix products: 7.82 us -> none  [the longest x3 4.41 us: pair_scores(): jnp.einsum('iltr,jlsr->ijlts', train[:, :, 1], val[:, :, 1], preferred_el...]
  transfers between devices with their start and end apart: 2 -> 0, of which waited for: 2 -> 0; matrix products, arithmetic and copies ran while one was open for 4% -> 0% of each run, Pallas kernels for 0% -> 0%
where the time goes in v3:
time: 112 us
  Pallas kernels  110 us (98%)
  local copies, waits for them, and re-layouts  1.3 us (1%)
    pallas_call x1, Pallas kernels, local(): pl.pallas_call(kernel, out_shape=jax.ShapeDtypeStruct((SUMS, 128), jnp.fl...  110 us

profile of v3, /device:TPU:24, one launch (start us, length us, event | category | flops | bytes accessed | tf_op | source)
XLA Modules:
  0.0 111.6 jit_solution(5560839391127761232)
XLA Ops:
  0.0 110.3 %score_ring.1 = f32[16,128]{1,0:T(8,128)} custom-call(bf16[12,2,64,1024]{3,2,1,0:T(8,128)(2,1)} %bitcast.4, bf16[4,2,64,1024]{3,2,1,0:T(8,128)(2,1)} %bitcast.5), custom_call_target="tpu_custom_call" | custom-call | tf_op jit(solution)/shard_map/score_ring/pallas_call | solution.py:321
  110.3 1.3 %reshape.11 = f32[3,4,12]{2,1,0:T(4,128)} reshape(f32[12,12]{1,0:T(8,128)} %bitcast.6) | data formatting | bytes 1152 | tf_op jit(solution)/shard_map/reshape | solution.py:356

commit v4 on v3

--- a/solution.py
+++ b/solution.py
@@ -19,11 +19,12 @@
 UP, DOWN = 0, 1
 OWN, OTHER = 0, 1
 CHUNKS = [(p, g) for p in range(2) for g in range(2)]
-TURNED = {UP: [(1, 0), (1, 1)], DOWN: [(1, 1)]}
+TURNED = {UP: [(0, 1), (1, 0), (1, 1)], DOWN: [(1, 0), (1, 1)]}
 TURN_AT = {UP: LAYERS, DOWN: RING - 1}
 TURNS = max(len(TURNED[UP]), len(TURNED[DOWN]), 1)
-HEAD = 2
-ORDER = {UP: [(OWN, 0, 0), (OWN, 0, 1), (OTHER, 0, 0), (OTHER, 0, 1), (OTHER, 1, 0), (OTHER, 1, 1), (OWN, 1, 0), (OWN, 1, 1)], DOWN: [(OWN, 0, 0), (OWN, 0, 1), (OTHER, 0, 0), (OTHER, 0, 1), (OWN, 1, 0), (OWN, 1, 1), (OTHER, 1, 0), (OTHER, 1, 1)]}
+HEAD = 1
+ORDER = {UP: [(OWN, 0), (OTHER, 0), (OTHER, 1), (OWN, 1)], DOWN: [(OWN, 0), (OTHER, 0), (OWN, 1), (OTHER, 1)]}
+BOTH = pl.ds(0, 2)
 
 
 def chip(column, z, core):
@@ -92,41 +93,53 @@
     def ring(step, d, which, p, g):
         first = isinstance(step, int) and step == 0
         src = val.at[2 * d + p, g] if first and which == OWN else held.at[step, which, p, g]
-        on_core, received = d, recv_sem.at[step, which, p, g]
+        sem = 1 if isinstance(g, int) else 0
+        on_core, received = d, recv_sem.at[step, which, p, sem]
         if isinstance(step, int) and step == LAST:
             dst = last.at[p, g, quarter((2 if which == d else 0) + d)]
+            received = recv_sem.at[step, which, p, g]
+            sem = g
             if d == DOWN and which == OTHER:
                 on_core, received = 0, cross_recv.at[p, g]
         else:
             dst = held.at[step + 1, which, p, g]
-        return remote(src, dst, send_sem.at[step, which, p, g], received, target(step, d, on_core))
+        return remote(src, dst, send_sem.at[step, which, p, sem], received, target(step, d, on_core))
 
     def starts_at(step, d):
         return lax.rem(z - step + RING, RING) if d == UP else lax.rem(z + step, RING)
 
-    def unless_turned(step, d, which, p, g, use):
-        other_way = 1 - d
-        if which == d and (p, g) in TURNED[other_way]:
-            pl.when(starts_at(step, d) != TURN_AT[other_way])(use)
+    def goes(step, d, which, p, use):
+        left = [g for g in range(2) if which != d or (p, g) not in TURNED[1 - d]]
+        if len(left) == 2:
+            use(BOTH)
+        else:
+            turns = starts_at(step, d) == TURN_AT[1 - d]
+            pl.when(jnp.logical_not(turns))(lambda: use(BOTH))
+            for g in left:
+                pl.when(turns)(lambda: use(g))
+
+    def ends(step, d, which, p, g, use):
+        if which == d and (p, g) in TURNED[1 - d]:
+            pl.when(starts_at(step, d) != TURN_AT[1 - d])(use)
         else:
             use()
 
     def turn(i, step, d):
         p, g = TURNED[d][i]
         first = isinstance(step, int) and step == 0
-        ends = isinstance(step, int) and step == LAST
+        final = isinstance(step, int) and step == LAST
         here = last.at[p, g, quarter(3 if d == UP else 2)]
         if first:
             src = val.at[2 + p, g] if d == UP else here
         else:
             src = turned.at[i]
         return remote(
-            src, here if ends else turned.at[i], turned_send.at[i], turned_recv.at[i], target(step, d, 0 if ends else d)
+            src, here if final else turned.at[i], turned_send.at[i], turned_recv.at[i], target(step, d, 0 if final else d)
         )
 
-    def stage(p, g):
+    def stage(p):
         half = 2 * (1 - core) + p
-        return remote(val.at[half, g], held.at[0, OTHER, p, g], stage_send.at[p, g], stage_recv.at[p, g], sibling)
+        return remote(val.at[half], held.at[0, OTHER, p], stage_send.at[p], stage_recv.at[p], sibling)
 
     def give(p, g, d):
         return remote(
@@ -141,11 +154,11 @@
 
         @pl.when(core == d)
         def _():
-            for which, p, g in ORDER[d][:HEAD]:
-                unless_turned(0, d, which, p, g, lambda: ring(0, d, which, p, g).start())
-
-    for p, g in CHUNKS:
-        stage(p, g).start()
+            for which, p in ORDER[d][:HEAD]:
+                goes(0, d, which, p, lambda g: ring(0, d, which, p, g).start())
+
+    for p in range(2):
+        stage(p).start()
     loads = [pltpu.make_async_copy(val.at[:, g], own.at[g], load_sem.at[0, g]) for g in range(2)]
     loads += [pltpu.make_async_copy(train.at[:, g], tokens.at[g], load_sem.at[1, g]) for g in range(2)]
     for copy in loads:
@@ -155,10 +168,10 @@
 
         @pl.when(core == d)
         def _():
-            for which, p, g in ORDER[d][HEAD:]:
+            for which, p in ORDER[d][HEAD:]:
                 if which == OTHER:
-                    stage(p, g).wait_recv()
-                unless_turned(0, d, which, p, g, lambda: ring(0, d, which, p, g).start())
+                    stage(p).wait_recv()
+                goes(0, d, which, p, lambda g: ring(0, d, which, p, g).start())
             if d == UP:
                 for i in range(len(TURNED[UP])):
                     pl.when(z == TURN_AT[UP])(lambda: turn(i, 0, UP).start())
@@ -197,13 +210,13 @@
         @pl.when(core == d)
         def _():
             def step_body(step, carry):
-                for which, p, g in ORDER[d]:
-
-                    def send_on():
+                for which, p in ORDER[d]:
+
+                    def send_on(g):
                         ring(step - 1, d, which, p, g).wait_recv()
                         ring(step, d, which, p, g).start()
 
-                    unless_turned(step, d, which, p, g, send_on)
+                    goes(step, d, which, p, send_on)
                 for i in range(len(TURNED[d])):
 
                     @pl.when((starts_at(step, d) == TURN_AT[d]) & (z >= LAYERS))
@@ -213,19 +226,16 @@
 
                 @pl.when(step >= 3)
                 def _():
-                    for which, p, g in ORDER[d]:
-                        unless_turned(step - 2, d, which, p, g, lambda: ring(step - 2, d, which, p, g).wait_send())
+                    for which, p in ORDER[d]:
+                        goes(step - 2, d, which, p, lambda g: ring(step - 2, d, which, p, g).wait_send())
 
                 return carry
 
             lax.fori_loop(1, LAST, step_body, 0)
-            for which, p, g in ORDER[d]:
-
-                def send_on():
-                    ring(LAST - 1, d, which, p, g).wait_recv()
-                    ring(LAST, d, which, p, g).start()
-
-                unless_turned(LAST, d, which, p, g, send_on)
+            for which, p in ORDER[d]:
+                goes(LAST, d, which, p, lambda g: ring(LAST - 1, d, which, p, g).wait_recv())
+                for g in range(2):
+                    ends(LAST, d, which, p, g, lambda: ring(LAST, d, which, p, g).start())
             for i in range(len(TURNED[d])):
 
                 @pl.when(z == (TURN_AT[d] + (LAST if d == UP else -LAST)))
@@ -233,19 +243,25 @@
                     turn(i, 1, d).wait_recv()
                     turn(i, LAST, d).start()
 
+    def pass_on(d, p):
+        for g in range(2):
+            ring(LAST, d, OTHER if d == UP else OWN, p, g).wait_recv()
+            hand_over(d, p, g).start()
+
     for p in range(2):
 
-        @pl.when(core == 0)
-        def _():
-            for g in range(2):
-                ring(LAST, UP, OTHER, p, g).wait_recv()
-                hand_over(UP, p, g).start()
+        @pl.when((core == 0) & ((z != 0) if p else (z >= 0)))
+        def _():
+            pass_on(UP, p)
+
+        if p == 0:
+            @pl.when((core == 0) & (z == 0))
+            def _():
+                pass_on(UP, 1)
 
         @pl.when(core == 1)
         def _():
-            for g in range(2):
-                ring(LAST, DOWN, OWN, p, g).wait_recv()
-                hand_over(DOWN, p, g).start()
+            pass_on(DOWN, p)
 
         for g in range(2):
 
@@ -289,9 +305,11 @@
 
         @pl.when(core == d)
         def _():
-            for step in (0, LAST - 2, LAST - 1, LAST):
-                for which, p, g in ORDER[d]:
-                    unless_turned(step, d, which, p, g, lambda: ring(step, d, which, p, g).wait_send())
+            for which, p in ORDER[d]:
+                for step in (0, LAST - 2, LAST - 1):
+                    goes(step, d, which, p, lambda g: ring(step, d, which, p, g).wait_send())
+                for g in range(2):
+                    ends(LAST, d, which, p, g, lambda: ring(LAST, d, which, p, g).wait_send())
             for p, g in CHUNKS:
                 hand_over(d, p, g).wait_send()
             if d == UP:
@@ -301,8 +319,8 @@
             for i in range(len(TURNED[d])):
                 pl.when(z >= LAYERS)(lambda: turn(i, 0, d).wait_send())
 
-    for p, g in CHUNKS:
-        stage(p, g).wait_send()
+    for p in range(2):
+        stage(p).wait_send()
 
     for peer in range(LAYERS):
 
@@ -333,8 +351,8 @@
             pltpu.VMEM((SUMS, 128), jnp.float32),
             pltpu.VMEM((LAYERS, SUMS, 128), jnp.float32),
             dma((2, 2)),
-            dma((2, 2)),
-            dma((2, 2)),
+            dma((2,)),
+            dma((2,)),
             dma((2, 2, 2)),
             dma((2, 2, 2)),
             dma((LAST + 1, 2, 2, 2)),
@@ -348,7 +366,7 @@
             dma((LAYERS,)),
         ],
         compiler_params=pltpu.CompilerParams(
-            collective_id=0, has_side_effects=True, vmem_limit_bytes=60 * 2**20
+            collective_id=0, has_side_effects=True, vmem_limit_bytes=53 * 2**20
         ),
         name="score_ring",
     )(train, val)

time: 112 us -> 110 us (0.982)
  no operation moved by 1% of the time
where the time goes in v4:
time: 110 us
  Pallas kernels  110 us (100%)
    pallas_call x1, Pallas kernels, local(): pl.pallas_call(kernel, out_shape=jax.ShapeDtypeStruct((SUMS, 128), jnp.fl...  110 us

profile of v4, /device:TPU:24, one launch (start us, length us, event | category | flops | bytes accessed | tf_op | source)
XLA Modules:
  0.0 110.2 jit_solution(7329161994169268925)
XLA Ops:
  0.0 109.6 %score_ring.1 = f32[16,128]{1,0:T(8,128)S(1)} custom-call(bf16[12,2,64,1024]{3,2,1,0:T(8,128)(2,1)} %bitcast.5, bf16[4,2,64,1024]{3,2,1,0:T(8,128)(2,1)} %bitcast.6), custom_call_target="tpu_custom_call" | custom-call | tf_op jit(solution)/shard_map/score_ring/pallas_call | solution.py:339
  109.6 0.6 reshape.11

commit v5 on v4

--- a/solution.py
+++ b/solution.py
@@ -19,8 +19,7 @@
 UP, DOWN = 0, 1
 OWN, OTHER = 0, 1
 CHUNKS = [(p, g) for p in range(2) for g in range(2)]
-TURNED = {UP: [(0, 1), (1, 0), (1, 1)], DOWN: [(1, 0), (1, 1)]}
-TURN_AT = {UP: LAYERS, DOWN: RING - 1}
+TURNED = {UP: [(8, 0, 1), (8, 1, 0), (8, 1, 1)], DOWN: [(15, 1, 0), (15, 1, 1)]}
 TURNS = max(len(TURNED[UP]), len(TURNED[DOWN]), 1)
 HEAD = 1
 ORDER = {UP: [(OWN, 0), (OTHER, 0), (OTHER, 1), (OWN, 1)], DOWN: [(OWN, 0), (OTHER, 0), (OWN, 1), (OTHER, 1)]}
@@ -109,23 +108,35 @@
         return lax.rem(z - step + RING, RING) if d == UP else lax.rem(z + step, RING)
 
     def goes(step, d, which, p, use):
-        left = [g for g in range(2) if which != d or (p, g) not in TURNED[1 - d]]
-        if len(left) == 2:
+        away = {}
+        if which == d:
+            for start, turned_p, g in TURNED[1 - d]:
+                if turned_p == p:
+                    away.setdefault(start, []).append(g)
+        if not away:
             use(BOTH)
-        else:
-            turns = starts_at(step, d) == TURN_AT[1 - d]
-            pl.when(jnp.logical_not(turns))(lambda: use(BOTH))
-            for g in left:
-                pl.when(turns)(lambda: use(g))
+            return
+        start_here = starts_at(step, d)
+        whole = start_here >= 0
+        for start, gone in away.items():
+            whole &= start_here != start
+            for g in range(2):
+                if g not in gone:
+                    pl.when(start_here == start)(lambda: use(g))
+        pl.when(whole)(lambda: use(BOTH))
 
     def ends(step, d, which, p, g, use):
-        if which == d and (p, g) in TURNED[1 - d]:
-            pl.when(starts_at(step, d) != TURN_AT[1 - d])(use)
+        goes_round = starts_at(step, d) >= 0
+        away = [start for start, turned_p, turned_g in TURNED[1 - d] if which == d and (turned_p, turned_g) == (p, g)]
+        for start in away:
+            goes_round &= starts_at(step, d) != start
+        if away:
+            pl.when(goes_round)(use)
         else:
             use()
 
     def turn(i, step, d):
-        p, g = TURNED[d][i]
+        _, p, g = TURNED[d][i]
         first = isinstance(step, int) and step == 0
         final = isinstance(step, int) and step == LAST
         here = last.at[p, g, quarter(3 if d == UP else 2)]
@@ -174,7 +185,7 @@
                 goes(0, d, which, p, lambda g: ring(0, d, which, p, g).start())
             if d == UP:
                 for i in range(len(TURNED[UP])):
-                    pl.when(z == TURN_AT[UP])(lambda: turn(i, 0, UP).start())
+                    pl.when(z == TURNED[UP][i][0])(lambda: turn(i, 0, UP).start())
                 for half in range(2):
                     for p, g in CHUNKS:
                         give(p, g, half).start()
@@ -182,7 +193,7 @@
                 for p, g in CHUNKS:
                     give(p, g, 0).wait_recv()
                 for i in range(len(TURNED[DOWN])):
-                    pl.when(z == TURN_AT[DOWN])(lambda: turn(i, 0, DOWN).start())
+                    pl.when(z == TURNED[DOWN][i][0])(lambda: turn(i, 0, DOWN).start())
 
     total[...] = jnp.zeros_like(total)
 
@@ -219,7 +230,7 @@
                     goes(step, d, which, p, send_on)
                 for i in range(len(TURNED[d])):
 
-                    @pl.when((starts_at(step, d) == TURN_AT[d]) & (z >= LAYERS))
+                    @pl.when(starts_at(step, d) == TURNED[d][i][0])
                     def _():
                         turn(i, step, d).wait_recv()
                         turn(i, step, d).start()
@@ -238,10 +249,29 @@
                     ends(LAST, d, which, p, g, lambda: ring(LAST, d, which, p, g).start())
             for i in range(len(TURNED[d])):
 
-                @pl.when(z == (TURN_AT[d] + (LAST if d == UP else -LAST)))
+                @pl.when(starts_at(LAST, d) == TURNED[d][i][0])
                 def _():
                     turn(i, 1, d).wait_recv()
                     turn(i, LAST, d).start()
+
+    def clear(steps):
+        for d in range(2):
+
+            @pl.when(core == d)
+            def _():
+                for which, p in ORDER[d]:
+                    for step in steps:
+                        goes(step, d, which, p, lambda g: ring(step, d, which, p, g).wait_send())
+
+    clear((0, LAST - 2))
+    for p in range(2):
+        stage(p).wait_send()
+
+    @pl.when(core == 0)
+    def _():
+        for p, g in CHUNKS:
+            for half in range(2):
+                give(p, g, half).wait_send()
 
     def pass_on(d, p):
         for g in range(2):
@@ -263,21 +293,22 @@
         def _():
             pass_on(DOWN, p)
 
+        if p == 1:
+            clear((LAST - 1,))
+
         for g in range(2):
 
             @pl.when(core == 0)
             def _():
                 hand_over(DOWN, p, g).wait_recv()
-                for way in (DOWN, UP):
-                    which = OTHER if way == DOWN else OWN
-                    other_way = 1 - way
-                    if (p, g) in TURNED[other_way]:
-                        ends = 0 if other_way == UP else LAYERS - 1
-                        i = TURNED[other_way].index((p, g))
-                        pl.when(z == ends)(lambda: turn(i, LAST, other_way).wait_recv())
-                        pl.when(z != ends)(lambda: ring(LAST, way, which, p, g).wait_recv())
-                    else:
-                        ring(LAST, way, which, p, g).wait_recv()
+                for way, which in ((DOWN, OTHER), (UP, OWN)):
+                    straight = z >= 0
+                    for i, (start, turned_p, turned_g) in enumerate(TURNED[1 - way]):
+                        if (turned_p, turned_g) == (p, g):
+                            here = z == (start + LAYERS) % RING
+                            straight &= jnp.logical_not(here)
+                            pl.when(here)(lambda: turn(i, LAST, 1 - way).wait_recv())
+                    pl.when(straight)(lambda: ring(LAST, way, which, p, g).wait_recv())
 
             @pl.when(core == 1)
             def _():
@@ -306,21 +337,14 @@
         @pl.when(core == d)
         def _():
             for which, p in ORDER[d]:
-                for step in (0, LAST - 2, LAST - 1):
-                    goes(step, d, which, p, lambda g: ring(step, d, which, p, g).wait_send())
                 for g in range(2):
                     ends(LAST, d, which, p, g, lambda: ring(LAST, d, which, p, g).wait_send())
             for p, g in CHUNKS:
                 hand_over(d, p, g).wait_send()
-            if d == UP:
-                for p, g in CHUNKS:
-                    for half in range(2):
-                        give(p, g, half).wait_send()
             for i in range(len(TURNED[d])):
-                pl.when(z >= LAYERS)(lambda: turn(i, 0, d).wait_send())
-
-    for p in range(2):
-        stage(p).wait_send()
+                past = z - TURNED[d][i][0] if d == UP else TURNED[d][i][0] - z
+                pl.when(lax.rem(past + RING, RING) <= LAST)(lambda: turn(i, 0, d).wait_send())
+
 
     for peer in range(LAYERS):
 

time: 110 us -> 110 us (level)
  no operation moved by 1% of the time
where the time goes in v5:
time: 110 us
  Pallas kernels  110 us (100%)
    pallas_call x1, Pallas kernels, local(): pl.pallas_call(kernel, out_shape=jax.ShapeDtypeStruct((SUMS, 128), jnp.fl...  110 us

profile of v5, /device:TPU:24, one launch (start us, length us, event | category | flops | bytes accessed | tf_op | source)
XLA Modules:
  0.0 110.2 jit_solution(18089547967695418794)
XLA Ops:
  0.0 109.6 %score_ring.1 = f32[16,128]{1,0:T(8,128)S(1)} custom-call(bf16[12,2,64,1024]{3,2,1,0:T(8,128)(2,1)} %bitcast.5, bf16[4,2,64,1024]{3,2,1,0:T(8,128)(2,1)} %bitcast.6), custom_call_target="tpu_custom_call" | custom-call | tf_op jit(solution)/shard_map/score_ring/pallas_call | solution.py:363
  109.6 0.6 reshape.11

commit v6 on v5

--- a/solution.py
+++ b/solution.py
@@ -353,7 +353,9 @@
             share(peer, peer).wait_recv()
             share(peer, layer).wait_send()
 
-    out[...] = jnp.sum(parts[...], axis=0)
+    sums = jnp.sum(parts[...], axis=0)
+    for hop in range(HOPS):
+        out[hop] = sums[hop * VAL_DEV : (hop + 1) * VAL_DEV, :TRAIN_DEV]
 
 
 def local(train_factors, val_factors):
@@ -362,7 +364,7 @@
     dma = pltpu.SemaphoreType.DMA
     summed = pl.pallas_call(
         kernel,
-        out_shape=jax.ShapeDtypeStruct((SUMS, 128), jnp.float32),
+        out_shape=jax.ShapeDtypeStruct((HOPS, VAL_DEV, TRAIN_DEV), jnp.float32),
         in_specs=[pl.BlockSpec(memory_space=pl.ANY)] * 2,
         out_specs=pl.BlockSpec(memory_space=pltpu.VMEM),
         scratch_shapes=[
@@ -394,8 +396,8 @@
         ),
         name="score_ring",
     )(train, val)
-    scores = summed[: HOPS * VAL_DEV, :TRAIN_DEV]
-    return scores.reshape(HOPS, VAL_DEV, TRAIN_DEV).transpose(2, 0, 1)
+
+    return summed.transpose(2, 0, 1)
 
 
 def solution(mesh):

time: 110 us -> 110 us (level)
  no operation moved by 1% of the time
where the time goes in v6:
time: 110 us
  Pallas kernels  110 us (100%)
    pallas_call x1, Pallas kernels, local(): pl.pallas_call(kernel, out_shape=jax.ShapeDtypeStruct((HOPS, VAL_DEV, TRA...  110 us

profile of v6, /device:TPU:24, one launch (start us, length us, event | category | flops | bytes accessed | tf_op | source)
XLA Modules:
  0.0 110.2 jit_solution(16211380752272647752)
XLA Ops:
  0.0 109.6 %score_ring.1 = f32[3,4,12]{2,1,0:T(4,128)S(1)} custom-call(bf16[12,2,64,1024]{3,2,1,0:T(8,128)(2,1)} %bitcast.4, bf16[4,2,64,1024]{3,2,1,0:T(8,128)(2,1)} %bitcast.5), custom_call_target="tpu_custom_call" | custom-call | tf_op jit(solution)/shard_map/score_ring/pallas_call | solution.py:365
  109.6 0.6 copy.4
